TPU v7x, 1024 devices: a whole 4x4x32 slice. The times are simulated.
1024 devices in a mesh: sec: 64 (over z_lo, x), mpo: 16 (over z_hi, y, core).
Axes of the slice: x: 4, y: 4, z: 32 (z_hi: 2, z_lo: 16; z = z_hi * 16 + z_lo), core: 2. Of those that a mesh axis runs over, the one named last changes fastest.
Arguments:
- wavefunction: bfloat16 [256, 256, 256], P('sec'), may hold values from -6 to 6
- left_env: bfloat16 [32, 128, 256, 256], P('mpo', 'sec'), may hold values from -0.1875 to 0.1875
- right_env: bfloat16 [32, 128, 256, 256], P('mpo', 'sec'), may hold values from -0.15625 to 0.15625
- pair_left: int32 [256], P('sec'), may hold values from 0 to 127, as said below
- pair_right: int32 [256], P('sec'), may hold values from 0 to 127, as said below
- mpo_mask: int32 [32, 256], P('mpo', 'sec'), may hold values 0 or 1
Outputs:
- applied: bfloat16 [256, 256, 256], P('sec')
Inputs may be any that keep to these rules, and one draw needn't show every extreme that they name: `pair_left`: the left sector of a pair in rows k * 4 to (k + 1) * 4 - 1 lies in sectors k * 2 to (k + 1) * 2 - 1. `pair_right`: the right sector of a pair in rows k * 4 to (k + 1) * 4 - 1 lies in sectors (k - 1) * 2 to (k + 2) * 2 - 1.
All inputs are finite; a program needn't handle non-finite values. No bound on the sum of `mpo_mask` on one device may be relied on, other than what follows from the above.
Results may differ from a plain program's by a relative error of at most 0.005.
Values may be sent and summed in bfloat16 or wider, within the bound.
A program may use at most 32 MiB of HBM per device.

v0:
```python
import jax
import jax.numpy as jnp
from jax import lax
from jax.sharding import PartitionSpec as P


def extended(shard, sides, width):
    for axis, dim in sides:
        size, length = (lax.axis_size(axis), shard.shape[dim])
        up = [(i, (i + 1) % size) for i in range(size - 1)]
        down = [(j, i) for i, j in up]
        last = lax.slice_in_dim(shard, length - width, length, axis=dim)
        first = lax.slice_in_dim(shard, 0, width, axis=dim)
        before = lax.ppermute(last, axis, up)
        after = lax.ppermute(first, axis, down)
        shard = jnp.concatenate([before, shard, after], axis=dim)
    return shard


def per_device(wavefunction, left_env, right_env, pair_left, pair_right, mpo_mask):
    sectors_here = left_env.shape[1]
    first_sector = lax.axis_index("sec") * sectors_here
    right_wide = extended(right_env, (("sec", 1),), sectors_here)
    left_local = pair_left - first_sector
    right_local = pair_right - first_sector + sectors_here
    left_sel = jnp.take(left_env, left_local, axis=1)
    right_sel = jnp.take(right_wide, right_local, axis=1)
    half = jnp.einsum(
        "wpij,pjk->wpik", left_sel, wavefunction, preferred_element_type=jnp.float32
    ).astype(jnp.bfloat16)
    half = half * mpo_mask.astype(jnp.bfloat16)[:, :, None, None]
    partial_sum = lax.dot_general(
        half, right_sel, (((0, 3), (0, 3)), ((1,), (1,))), preferred_element_type=jnp.float32
    )
    owned = lax.psum_scatter(partial_sum, "mpo", scatter_dimension=1, tiled=True).astype(
        jnp.bfloat16
    )
    return lax.all_gather(owned, "mpo", axis=1, tiled=True)


def solution(mesh):
    return jax.shard_map(
        per_device,
        mesh=mesh,
        in_specs=(
            P("sec", None, None),
            P("mpo", "sec", None, None),
            P("mpo", "sec", None, None),
            P("sec"),
            P("sec"),
            P("mpo", "sec"),
        ),
        out_specs=P("sec", None, None),
        check_vma=False,
    )
```

profile of v0, /device:TPU:1, one launch (start us, length us, event | category | flops | bytes accessed | tf_op | source)
XLA Modules:
  0.0 270.0 jit_solution(10585904733644897441)
XLA Ops:
  6.5 0.0 copy-start
  6.5 0.0 reduce-scatter.2.cloned.1.call-start
  6.5 4.1 %collective-permute-start = (bf16[2,2,256,256]{3,2,1,0:T(8,128)(2,1)}, bf16[2,2,256,256]{3,2,1,0:T(8,128)(2,1)S(1)}, u32[]{:S(2)}, u32[]{:S(2)}) collective-permute-start(bf16[2,2,256,256]{3,2,1,0:T(8,128)(2,1)} %param.8), channel_id=1, source_target_pairs={{0,16},{16,32},{32,48},{48,64},{64,80},{80,96},{96,112},{112,128},... | collective-permute-start | bytes 1572872 | tf_op jit(solution)/shard_map/ppermute | solution.py:14
  10.6 1.3 collective-permute-start.1
  12.0 0.7 convert_element_type.14
  12.6 0.1 copy.7
  12.7 0.7 compare_and_fusion
  13.4 0.0 copy-done
  13.4 0.6 gather_fusion
  14.1 3.0 %collective-permute-done = bf16[2,2,256,256]{3,2,1,0:T(8,128)(2,1)S(1)} collective-permute-done((bf16[2,2,256,256]{3,2,1,0:T(8,128)(2,1)}, bf16[2,2,256,256]{3,2,1,0:T(8,128)(2,1)S(1)}, u32[]{:S(2)}, u32[]{:S(2)}) %collective-permute-start) | collective-permute-done | bytes 524320 | tf_op jit(solution)/shard_map/ppermute | solution.py:14
  17.0 0.0 copy-start.1
  17.0 0.8 copy-done.1
  17.8 3.1 %collective-permute-done.1 = bf16[2,2,256,256]{3,2,1,0:T(8,128)(2,1)} collective-permute-done((bf16[2,2,256,256]{3,2,1,0:T(8,128)(2,1)}, bf16[2,2,256,256]{3,2,1,0:T(8,128)(2,1)}, u32[]{:S(2)}, u32[]{:S(2)}) %collective-permute-start.1) | collective-permute-done | bytes 524320 | tf_op jit(solution)/shard_map/ppermute | solution.py:15
  20.9 1.5 pad_maximum_fusion
  22.4 1.6 gather_fusion.1
  24.1 3.1 %convolution_bitcast_fusion = f32[4,256,256]{2,1,0:T(8,128)} fusion(bf16[4,2,256,256]{3,2,1,0:T(8,128)(2,1)} %gather_fusion.1, bf16[4,2,256,256]{3,2,1,0:T(8,128)(2,1)S(1)} %gather_fusion, pred[4]{0:T(512)(128)(4,1)S(1)} %get-tuple-element.7, pred[4]{0:T(512)(128)(4,1)S(1)} %get-tuple-element.9, bf16[4,256,256]{2,1,0:T(8,128)(2,1)} %param.6, ...), kind=kOutput, calls=%fused_computation.4 | convolution fusion | flops 538968064 | bytes 3670040 | tf_op jit(solution)/shard_map/dot_general | solution.py:32
  27.2 0.0 reduce-scatter.2.cloned.1.call-update
  27.2 175.6 %reduce-scatter.2.cloned.1.call-done = f32[4,16,256]{2,1,0:T(8,128)} async-done(((f32[4,256,256]{2,1,0:T(8,128)}), f32[4,16,256]{2,1,0:T(8,128)}) %reduce-scatter.2.cloned.1.call-update) | async-done | bytes 65552 | tf_op jit(solution)/shard_map/reduce_scatter | solution.py:35
  202.8 0.8 convert_element_type.15
  203.6 58.8 %all_gather.3 = bf16[4,256,256]{2,1,0:T(8,128)(2,1)S(1)} all-gather(bf16[4,16,256]{2,1,0:T(8,128)(2,1)S(1)} %convert_element_type.15), channel_id=1, replica_groups=mesh['sec'=64,'mpo'=16] {'mpo'}, dimensions={1}, use_global_device_ids=true | all-gather | bytes 557056 | tf_op jit(solution)/shard_map/all_gather | solution.py:38
  262.4 0.8 copy.11
  (2 shorter events, 0.0 us)
Async XLA Ops:
  6.5 6.9 %copy-start = (bf16[2,2,256,256]{3,2,1,0:T(8,128)(2,1)S(1)}, bf16[2,2,256,256]{3,2,1,0:T(8,128)(2,1)}, u32[]{:S(2)}) copy-start(bf16[2,2,256,256]{3,2,1,0:T(8,128)(2,1)} %param.7) | copy-start | bytes 1572868
  6.5 196.2 %reduce-scatter.2.cloned.1.call-start = ((), (), s32[]{:S(2)}) async-start(), calls=%async_computation.1 | async-start | bytes 1114112 | tf_op jit(solution)/shard_map/reduce_scatter | solution.py:35
  6.5 10.5 %collective-permute-start = (bf16[2,2,256,256]{3,2,1,0:T(8,128)(2,1)}, bf16[2,2,256,256]{3,2,1,0:T(8,128)(2,1)S(1)}, u32[]{:S(2)}, u32[]{:S(2)}) collective-permute-start(bf16[2,2,256,256]{3,2,1,0:T(8,128)(2,1)} %param.8), channel_id=1, source_target_pairs={{0,16},{16,32},{32,48},{48,64},{64,80},{80,96},{96,112},{112,128},... | collective-permute-start | bytes 1572872 | tf_op jit(solution)/shard_map/ppermute | solution.py:14
  10.6 10.2 %collective-permute-start.1 = (bf16[2,2,256,256]{3,2,1,0:T(8,128)(2,1)}, bf16[2,2,256,256]{3,2,1,0:T(8,128)(2,1)}, u32[]{:S(2)}, u32[]{:S(2)}) collective-permute-start(bf16[2,2,256,256]{3,2,1,0:T(8,128)(2,1)} %param.8), channel_id=1, source_target_pairs={{16,0},{32,16},{48,32},{64,48},{80,64},{96,80},{112,96},{128,112},... | collective-permute-start | bytes 1572872 | tf_op jit(solution)/shard_map/ppermute | solution.py:15
  17.0 0.8 copy-start.1
Sparse Core Ops, SparseCore 0:
  27.3 175.3 reduce-scatter.1
where the time goes:
time: 273 us; the launch traced here: 270 us
  waiting for transfers between devices  182 us (67%)
  blocking collectives  58.8 us (22%)
  between operations  13.4 us (5%)
  starting transfers between devices  5.39 us (2%)
  local copies, waits for them, and re-layouts  3.95 us (1%)
  other arithmetic  3.75 us (1%)
  matrix products  3.13 us (1%)
    reduce_scatter x1, waiting for transfers between devices, per_device(): lax.psum_scatter(partial_sum, 'mpo', scatter_dimension=1, tiled=True)  176 us
    all_gather x1, blocking collectives, per_device(): return lax.all_gather(owned, 'mpo', axis=1, tiled=True)  58.8 us
  transfers between devices with their start and end apart: 3, of which 3 were waited for; matrix products, arithmetic and copies ran while one was open for 1% of the time, Pallas kernels for 0%

commit v1 on v0

v1 whole, which is shorter than its diff:
```python
import functools

import jax
import jax.numpy as jnp
from jax import lax
from jax.experimental import pallas as pl
from jax.experimental.pallas import tpu as pltpu
from jax.sharding import PartitionSpec as P

X = 4
CHUNKS = 4
FAR = "z4"
F32, BF16 = jnp.float32, jnp.bfloat16


def kernel(
    n_sec, n_mpo, pairs, left_ix, right_ix, mask,
    psi_hbm, left_hbm, right_hbm, out,
    psi, left, half, part, got, mine, twin, full, *rest,
):
    C = CHUNKS
    G = n_mpo // 2
    z_lo_size = n_sec // X
    ring = 2 * z_lo_size
    wide = rest[:C]
    (in_sem, own_sem, r_send, r_recv, s_send, s_recv, z_send, z_recv, g_send, g_recv, near_sem, far_sem) = rest[C:]
    W, S = left.shape[0], left.shape[1]
    B = psi.shape[-1]
    lc = B // C
    per = 128 // lc
    groups = pairs // per
    rows = B // G

    sec, mpo = lax.axis_index("sec"), lax.axis_index("mpo")
    z_hi, me = mpo // G, mpo % G
    z_lo, x = sec // X, sec % X

    def along_z(step):
        z = lax.rem(z_hi * z_lo_size + z_lo + step + ring, ring)
        return lax.rem(z, z_lo_size) * X + x, (z // z_lo_size) * G + me

    def in_plane(step):
        return sec, z_hi * G + lax.rem(me + step, G)

    has_low, has_high = sec > 0, sec < n_sec - 1
    far = {"z16": (ring // 2,), "z8": (ring // 4, -(ring // 4)), "z4": (ring // 8, -(ring // 8))}[FAR]

    def signal(sem, device):
        pl.semaphore_signal(sem, inc=1, device_id=device, device_id_type=pl.DeviceIdType.MESH)

    def remote(src, dst, send, recv, device):
        return pltpu.make_async_remote_copy(
            src_ref=src, dst_ref=dst, send_sem=send, recv_sem=recv,
            device_id=device, device_id_type=pl.DeviceIdType.MESH,
        )

    barrier = pltpu.get_barrier_semaphore()
    for step in far:
        signal(barrier, along_z(step))
    pl.when(has_low)(lambda: signal(barrier, (sec - 1, mpo)))
    pl.when(has_high)(lambda: signal(barrier, (sec + 1, mpo)))
    for step in range(1, G):
        signal(barrier, in_plane(step))

    loads = [
        pltpu.make_async_copy(left_hbm, left, in_sem.at[0]),
        pltpu.make_async_copy(psi_hbm, psi, in_sem.at[1]),
    ]
    own = [
        pltpu.make_async_copy(right_hbm.at[:, :, pl.ds(c * lc, lc)], wide[c].at[:, pl.ds(S, S)], own_sem.at[c])
        for c in range(C)
    ]
    for copy in loads + own:
        copy.start()

    def to_low(c):
        return remote(right_hbm.at[:, :, pl.ds(c * lc, lc)], wide[c].at[:, pl.ds(2 * S, S)],
                      r_send.at[c, 0], r_recv.at[c, 0], (sec - 1, mpo))

    def to_high(c):
        return remote(right_hbm.at[:, :, pl.ds(c * lc, lc)], wide[c].at[:, pl.ds(0, S)],
                      r_send.at[c, 1], r_recv.at[c, 1], (sec + 1, mpo))

    first = sec * S
    left_at = [jnp.clip(left_ix[p] - first, 0, S - 1) for p in range(pairs)]
    right_at = [jnp.clip(right_ix[p] - first + S, 0, 3 * S - 1) for p in range(pairs)]

    def halves():
        for copy in loads:
            copy.wait()
        for p in range(pairs):
            for w in range(W):
                block = jnp.dot(left[w, left_at[p]], psi[p], preferred_element_type=F32)
                half[w, p] = (block * mask[w, p].astype(F32)).astype(BF16)

    if FAR == "z16":
        halves()
    pl.semaphore_wait(barrier, has_low.astype(jnp.int32) + has_high.astype(jnp.int32) + (G - 1 + len(far)))

    for c in range(C):
        pl.when(has_low)(lambda c=c: to_low(c).start())
        pl.when(has_high)(lambda c=c: to_high(c).start())
    if FAR == "z8":
        signal(far_sem, along_z(-(ring // 4)))
    if FAR == "z4":
        signal(near_sem, along_z(ring // 8))
        signal(near_sem, along_z(-(ring // 8)))
    if FAR != "z16":
        halves()

    sends = []

    def contract(c):
        own[c].wait()
        pl.when(has_high)(lambda: to_low(c).wait_recv())
        pl.when(has_low)(lambda: to_high(c).wait_recv())
        lane = lax.broadcasted_iota(jnp.int32, (B, 128), 1)
        for group in range(groups):
            members = range(group * per, (group + 1) * per)
            sums = [None] * per
            for w in range(W):
                rights = jnp.concatenate([wide[c][w, right_at[p]] for p in members], axis=0)
                for q, p in enumerate(members):
                    term = lax.dot_general(half[w, p], rights, (((1,), (1,)), ((), ())), preferred_element_type=F32)
                    sums[q] = term if sums[q] is None else sums[q] + term
            block = sums[0]
            for q in range(1, per):
                block = jnp.where(lane < q * lc, block, sums[q])
            part[c, :, group] = block.astype(BF16).reshape(G, rows, 128)
        for step in range(1, G):
            copy = remote(part.at[c, lax.rem(me + step, G)], got.at[c, step - 1],
                          s_send.at[c, step - 1], s_recv.at[c, step - 1], in_plane(step))
            copy.start()
            sends.append(copy)

    def twin_copy(c):
        return remote(mine.at[c], twin.at[c], z_send.at[c], z_recv.at[c], along_z(ring // 2))

    def add_up(c):
        total = part[c, me].astype(F32)
        for step in range(1, G):
            remote(part.at[c, 0], got.at[c, step - 1], s_send.at[c, step - 1], s_recv.at[c, step - 1],
                   in_plane(step)).wait_recv()
            total = total + got[c, step - 1].astype(F32)
        mine[c] = total.astype(BF16)
        copy = twin_copy(c)
        copy.start()
        sends.append(copy)

    def hand_back(c):
        twin_copy(c).wait_recv()
        full[c, me] = (mine[c].astype(F32) + twin[c].astype(F32)).astype(BF16)
        for step in range(1, G):
            copy = remote(full.at[c, me], full.at[c, me], g_send.at[c, step - 1], g_recv.at[c, step - 1], in_plane(step))
            copy.start()
            sends.append(copy)

    def place(c):
        for step in range(1, G):
            source = lax.rem(me - step + G, G)
            remote(full.at[c, source], full.at[c, source], g_send.at[c, step - 1], g_recv.at[c, step - 1],
                   in_plane(step)).wait_recv()
        if per == 1:
            for p in range(pairs):
                out[p, :, pl.ds(c * 128, 128)] = full[c, :, p].reshape(B, 128)
        elif c % per == per - 1:
            chunks = range(c - per + 1, c + 1)
            for group in range(groups):
                blocks = [full[k, :, group].reshape(B, 128) for k in chunks]
                for q in range(per):
                    out[group * per + q, :, pl.ds(c // per * 128, 128)] = jnp.concatenate(
                        [b[:, q * lc:(q + 1) * lc] for b in blocks], axis=1
                    )

    for c in range(C):
        contract(c)
        if c == 0 and FAR == "z4":
            pl.semaphore_wait(near_sem, 2)
            signal(far_sem, along_z(-(ring // 4)))
        if c == 1:
            if FAR != "z16":
                pl.semaphore_wait(far_sem, 1)
        if c > 0:
            add_up(c - 1)
    add_up(C - 1)
    for c in range(C):
        hand_back(c)
        if c > 0:
            place(c - 1)
    place(C - 1)

    for c in range(C):
        pl.when(has_low)(lambda c=c: to_low(c).wait_send())
        pl.when(has_high)(lambda c=c: to_high(c).wait_send())
    for copy in sends:
        copy.wait_send()


def per_device(n_sec, n_mpo, wavefunction, left_env, right_env, pair_left, pair_right, mpo_mask):
    pairs, B, _ = wavefunction.shape
    W, S = left_env.shape[:2]
    G = n_mpo // 2
    C = CHUNKS
    lc = B // C
    groups = pairs * lc // 128
    rows = B // G
    piece = (groups, rows, 128)
    smem = pl.BlockSpec(memory_space=pltpu.SMEM)
    hbm = pl.BlockSpec(memory_space=pl.ANY)
    dma = pltpu.SemaphoreType.DMA
    return pl.pallas_call(
        functools.partial(kernel, n_sec, n_mpo, pairs),
        out_shape=jax.ShapeDtypeStruct(wavefunction.shape, BF16),
        in_specs=[smem, smem, smem, hbm, hbm, hbm],
        out_specs=pl.BlockSpec(memory_space=pltpu.VMEM),
        scratch_shapes=[
            pltpu.VMEM((pairs, B, B), BF16),
            pltpu.VMEM((W, S, B, B), BF16),
            pltpu.VMEM((W, pairs, B, B), BF16),
            pltpu.VMEM((C, G) + piece, BF16),
            pltpu.VMEM((C, G - 1) + piece, BF16),
            pltpu.VMEM((C,) + piece, BF16),
            pltpu.VMEM((C,) + piece, BF16),
            pltpu.VMEM((C, G) + piece, BF16),
        ]
        + [pltpu.VMEM((W, 3 * S, lc, B), BF16)] * C
        + [
            dma((2,)), dma((C,)), dma((C, 2)), dma((C, 2)),
            dma((C, G - 1)), dma((C, G - 1)), dma((C,)), dma((C,)),
            dma((C, G - 1)), dma((C, G - 1)),
            pltpu.SemaphoreType.REGULAR, pltpu.SemaphoreType.REGULAR,
        ],
        compiler_params=pltpu.CompilerParams(collective_id=0, has_side_effects=True, vmem_limit_bytes=58 * 2**20),
        cost_estimate=pl.CostEstimate(flops=8 * W * pairs * B**3 // 2, bytes_accessed=8 * pairs * B * B, transcendentals=0),
    )(pair_left, pair_right, mpo_mask, wavefunction, left_env, right_env)


def solution(mesh):
    return jax.shard_map(
        functools.partial(per_device, mesh.shape["sec"], mesh.shape["mpo"]),
        mesh=mesh,
        in_specs=(
            P("sec", None, None),
            P("mpo", "sec", None, None),
            P("mpo", "sec", None, None),
            P("sec"),
            P("sec"),
            P("mpo", "sec"),
        ),
        out_specs=P("sec", None, None),
        check_vma=False,
    )
```

time: 273 us -> 64.3 us (0.24)
  waiting for transfers between devices: 182 us -> 0 us
  Pallas kernels: 0 us -> 61.9 us
  blocking collectives: 58.8 us -> 0 us
  between operations: 13.4 us -> 0.01 us
  starting transfers between devices: 5.39 us -> 0 us
  other arithmetic: 3.75 us -> 0 us
  matrix products: 3.13 us -> 0 us
    reduce_scatter x1 -> x0, waiting for transfers between devices: 176 us -> none  [per_device(): lax.psum_scatter(partial_sum, 'mpo', scatter_dimension=1, tiled=True)]
    pallas_call x0 -> x1, Pallas kernels: none -> 61.9 us  [per_device(): pl.pallas_call(functools.partial(kernel, n_sec, n_mpo, pairs), out_shape=...]
    all_gather x1 -> x0, blocking collectives: 58.8 us -> none  [per_device(): return lax.all_gather(owned, 'mpo', axis=1, tiled=True)]
    ppermute x2 -> x0, waiting for transfers between devices: 6.02 us -> none  [the longest x1 3.06 us: extended(): after = lax.ppermute(first, axis, down)]
    ppermute x2 -> x0, starting transfers between devices: 5.39 us -> none  [the longest x1 4.1 us: extended(): before = lax.ppermute(last, axis, up)]
    dot_general x1 -> x0, matrix products: 3.13 us -> none  [per_device(): lax.dot_general(half, right_sel, (((0, 3), (0, 3)), ((1,), (1,))), prefer...]
  transfers between devices with their start and end apart: 3 -> 0, of which waited for: 3 -> 0; matrix products, arithmetic and copies ran while one was open for 1% -> 0% of each run, Pallas kernels for 0% -> 0%
where the time goes in v1:
time: 64.3 us; the launch traced here: 63.8 us
  Pallas kernels  61.9 us (96%)
  local copies, waits for them, and re-layouts  1.87 us (3%)
    pallas_call x1, Pallas kernels, per_device(): pl.pallas_call(functools.partial(kernel, n_sec, n_mpo, pairs), out_shape=...  61.9 us
    unnamed x1, local copies, waits for them, and re-layouts  1.87 us

profile of v1, /device:TPU:1, one launch (start us, length us, event | category | flops | bytes accessed | tf_op | source)
XLA Modules:
  0.0 63.8 jit_solution(3932989634499621412)
XLA Ops:
  0.0 61.9 %shard_map.64 = bf16[4,256,256]{2,1,0:T(8,128)(2,1)} custom-call(s32[4]{0:T(128)} %left_ix.1, s32[4]{0:T(128)} %right_ix.1, s32[2,4]{1,0:T(2,128)} %mask.1, bf16[4,256,256]{2,1,0:T(8,128)(2,1)} %psi_hbm.1, bf16[2,2,256,256]{3,2,1,0:T(8,128)(2,1)} %left_hbm.1, bf16[2,2,256,256]{3,2,1,0:T(8,128)(2,1)} %right_hbm.1), custom_call_target="tpu_custom_call" | custom-call | flops 536870912 | bytes 2097152 | tf_op jit(solution)/shard_map/pallas_call | solution.py:211
  61.9 1.9 %copy.8 = bf16[4,256,256]{2,1,0:T(8,128)(2,1)} copy(bf16[4,256,256]{2,1,0:T(8,128)(2,1)} %shard_map.64) | data formatting | bytes 1048576

commit v2 on v1

--- a/solution.py
+++ b/solution.py
@@ -9,21 +9,22 @@
 
 X = 4
 CHUNKS = 4
-FAR = "z4"
+REPLY = 12
+LEAD = 2
 F32, BF16 = jnp.float32, jnp.bfloat16
 
 
 def kernel(
-    n_sec, n_mpo, pairs, left_ix, right_ix, mask,
+    n_sec, n_mpo, pairs, left_ix_hbm, right_ix_hbm, mask_hbm,
     psi_hbm, left_hbm, right_hbm, out,
-    psi, left, half, part, got, mine, twin, full, *rest,
+    left_ix, right_ix, mask, psi, left, half, part, got, mine, twin, full, *rest,
 ):
     C = CHUNKS
     G = n_mpo // 2
     z_lo_size = n_sec // X
     ring = 2 * z_lo_size
     wide = rest[:C]
-    (in_sem, own_sem, r_send, r_recv, s_send, s_recv, z_send, z_recv, g_send, g_recv, near_sem, far_sem) = rest[C:]
+    (in_sem, own_sem, r_send, r_recv, s_send, s_recv, z_send, z_recv, g_send, g_recv, far_sem) = rest[C:]
     W, S = left.shape[0], left.shape[1]
     B = psi.shape[-1]
     lc = B // C
@@ -43,7 +44,6 @@
         return sec, z_hi * G + lax.rem(me + step, G)
 
     has_low, has_high = sec > 0, sec < n_sec - 1
-    far = {"z16": (ring // 2,), "z8": (ring // 4, -(ring // 4)), "z4": (ring // 8, -(ring // 8))}[FAR]
 
     def signal(sem, device):
         pl.semaphore_signal(sem, inc=1, device_id=device, device_id_type=pl.DeviceIdType.MESH)
@@ -55,14 +55,16 @@
         )
 
     barrier = pltpu.get_barrier_semaphore()
-    for step in far:
-        signal(barrier, along_z(step))
+    pl.when(z_hi == 0)(lambda: signal(barrier, along_z(ring // 2)))
     pl.when(has_low)(lambda: signal(barrier, (sec - 1, mpo)))
     pl.when(has_high)(lambda: signal(barrier, (sec + 1, mpo)))
     for step in range(1, G):
         signal(barrier, in_plane(step))
 
     loads = [
+        pltpu.make_async_copy(left_ix_hbm, left_ix, in_sem.at[2]),
+        pltpu.make_async_copy(right_ix_hbm, right_ix, in_sem.at[3]),
+        pltpu.make_async_copy(mask_hbm, mask, in_sem.at[4]),
         pltpu.make_async_copy(left_hbm, left, in_sem.at[0]),
         pltpu.make_async_copy(psi_hbm, psi, in_sem.at[1]),
     ]
@@ -81,32 +83,24 @@
         return remote(right_hbm.at[:, :, pl.ds(c * lc, lc)], wide[c].at[:, pl.ds(0, S)],
                       r_send.at[c, 1], r_recv.at[c, 1], (sec + 1, mpo))
 
-    first = sec * S
-    left_at = [jnp.clip(left_ix[p] - first, 0, S - 1) for p in range(pairs)]
-    right_at = [jnp.clip(right_ix[p] - first + S, 0, 3 * S - 1) for p in range(pairs)]
-
     def halves():
         for copy in loads:
             copy.wait()
+        left_at = [jnp.clip(left_ix[p] - sec * S, 0, S - 1) for p in range(pairs)]
         for p in range(pairs):
             for w in range(W):
                 block = jnp.dot(left[w, left_at[p]], psi[p], preferred_element_type=F32)
                 half[w, p] = (block * mask[w, p].astype(F32)).astype(BF16)
 
-    if FAR == "z16":
-        halves()
-    pl.semaphore_wait(barrier, has_low.astype(jnp.int32) + has_high.astype(jnp.int32) + (G - 1 + len(far)))
+    pl.semaphore_wait(barrier, has_low.astype(jnp.int32) + has_high.astype(jnp.int32) + z_hi + (G - 1))
 
     for c in range(C):
         pl.when(has_low)(lambda c=c: to_low(c).start())
         pl.when(has_high)(lambda c=c: to_high(c).start())
-    if FAR == "z8":
-        signal(far_sem, along_z(-(ring // 4)))
-    if FAR == "z4":
-        signal(near_sem, along_z(ring // 8))
-        signal(near_sem, along_z(-(ring // 8)))
-    if FAR != "z16":
-        halves()
+    pl.when(z_hi == 1)(lambda: signal(far_sem, along_z(ring // 2)))
+    halves()
+    first = sec * S
+    right_at = [jnp.clip(right_ix[p] - first + S, 0, 3 * S - 1) for p in range(pairs)]
 
     sends = []
 
@@ -143,12 +137,13 @@
                    in_plane(step)).wait_recv()
             total = total + got[c, step - 1].astype(F32)
         mine[c] = total.astype(BF16)
-        copy = twin_copy(c)
-        copy.start()
-        sends.append(copy)
+        pl.when(z_hi == 1)(lambda: twin_copy(c).start())
 
     def hand_back(c):
         twin_copy(c).wait_recv()
+        for k in range(C):
+            if (k < LEAD and c == 0) or (k == c + LEAD - 1 and c > 0):
+                pl.when(jnp.logical_and(z_hi == 0, z_lo < REPLY))(lambda k=k: twin_copy(k).start())
         full[c, me] = (mine[c].astype(F32) + twin[c].astype(F32)).astype(BF16)
         for step in range(1, G):
             copy = remote(full.at[c, me], full.at[c, me], g_send.at[c, step - 1], g_recv.at[c, step - 1], in_plane(step))
@@ -174,15 +169,19 @@
 
     for c in range(C):
         contract(c)
-        if c == 0 and FAR == "z4":
-            pl.semaphore_wait(near_sem, 2)
-            signal(far_sem, along_z(-(ring // 4)))
-        if c == 1:
-            if FAR != "z16":
-                pl.semaphore_wait(far_sem, 1)
         if c > 0:
             add_up(c - 1)
     add_up(C - 1)
+
+    @pl.when(z_hi == 0)
+    def _():
+        pl.semaphore_wait(far_sem, 1)
+
+        @pl.when(z_lo >= REPLY)
+        def _():
+            for c in range(C):
+                twin_copy(c).start()
+
     for c in range(C):
         hand_back(c)
         if c > 0:
@@ -192,6 +191,7 @@
     for c in range(C):
         pl.when(has_low)(lambda c=c: to_low(c).wait_send())
         pl.when(has_high)(lambda c=c: to_high(c).wait_send())
+        twin_copy(c).wait_send()
     for copy in sends:
         copy.wait_send()
 
@@ -205,15 +205,17 @@
     groups = pairs * lc // 128
     rows = B // G
     piece = (groups, rows, 128)
-    smem = pl.BlockSpec(memory_space=pltpu.SMEM)
     hbm = pl.BlockSpec(memory_space=pl.ANY)
     dma = pltpu.SemaphoreType.DMA
     return pl.pallas_call(
         functools.partial(kernel, n_sec, n_mpo, pairs),
-        out_shape=jax.ShapeDtypeStruct(wavefunction.shape, BF16),
-        in_specs=[smem, smem, smem, hbm, hbm, hbm],
+        out_shape=pltpu.VMEM(wavefunction.shape, BF16),
+        in_specs=[hbm] * 6,
         out_specs=pl.BlockSpec(memory_space=pltpu.VMEM),
         scratch_shapes=[
+            pltpu.SMEM((pairs,), jnp.int32),
+            pltpu.SMEM((pairs,), jnp.int32),
+            pltpu.SMEM((W, pairs), jnp.int32),
             pltpu.VMEM((pairs, B, B), BF16),
             pltpu.VMEM((W, S, B, B), BF16),
             pltpu.VMEM((W, pairs, B, B), BF16),
@@ -225,10 +227,10 @@
         ]
         + [pltpu.VMEM((W, 3 * S, lc, B), BF16)] * C
         + [
-            dma((2,)), dma((C,)), dma((C, 2)), dma((C, 2)),
+            dma((5,)), dma((C,)), dma((C, 2)), dma((C, 2)),
             dma((C, G - 1)), dma((C, G - 1)), dma((C,)), dma((C,)),
             dma((C, G - 1)), dma((C, G - 1)),
-            pltpu.SemaphoreType.REGULAR, pltpu.SemaphoreType.REGULAR,
+            pltpu.SemaphoreType.REGULAR,
         ],
         compiler_params=pltpu.CompilerParams(collective_id=0, has_side_effects=True, vmem_limit_bytes=58 * 2**20),
         cost_estimate=pl.CostEstimate(flops=8 * W * pairs * B**3 // 2, bytes_accessed=8 * pairs * B * B, transcendentals=0),

time: 64.3 us -> 60.6 us (0.942)
  Pallas kernels: 61.9 us -> 59.6 us
  local copies, waits for them, and re-layouts: 1.87 us -> 0.8 us
    pallas_call x1, Pallas kernels: 61.9 us -> 59.6 us  [per_device(): pl.pallas_call(functools.partial(kernel, n_sec, n_mpo, pairs), out_shape=...]
    unnamed x1, local copies, waits for them, and re-layouts: 1.87 us -> 0.8 us
where the time goes in v2:
time: 60.6 us; the launch traced here: 60.4 us
  Pallas kernels  59.6 us (98%)
  local copies, waits for them, and re-layouts  0.8 us (1%)
    pallas_call x1, Pallas kernels, per_device(): pl.pallas_call(functools.partial(kernel, n_sec, n_mpo, pairs), out_shape=...  59.6 us

profile of v2, /device:TPU:1, one launch (start us, length us, event | category | flops | bytes accessed | tf_op | source)
XLA Modules:
  0.0 60.4 jit_solution(1836237687692058793)
XLA Ops:
  0.0 59.6 %shard_map.64 = bf16[4,256,256]{2,1,0:T(8,128)(2,1)S(1)} custom-call(s32[4]{0:T(128)} %left_ix_hbm.1, s32[4]{0:T(128)} %right_ix_hbm.1, s32[2,4]{1,0:T(2,128)} %mask_hbm.1, bf16[4,256,256]{2,1,0:T(8,128)(2,1)} %psi_hbm.1, bf16[2,2,256,256]{3,2,1,0:T(8,128)(2,1)} %left_hbm.1, bf16[2,2,256,256]{3,2,1,0:T(8,128)(2,1)} %right_hbm.1), custom_call_target="tpu_custom_call" | custom-call | flops 536870912 | bytes 2097152 | tf_op jit(solution)/shard_map/pallas_call | solution.py:210
  59.6 0.8 %copy.8 = bf16[4,256,256]{2,1,0:T(8,128)(2,1)} copy(bf16[4,256,256]{2,1,0:T(8,128)(2,1)S(1)} %shard_map.64) | data formatting | bytes 1048576

commit v3 on v2

--- a/solution.py
+++ b/solution.py
@@ -8,8 +8,10 @@
 from jax.sharding import PartitionSpec as P
 
 X = 4
-CHUNKS = 4
-REPLY = 12
+CHUNKS = (64, 64, 64, 64)
+REPLY = 8
+ANSWER = 1
+FLIP = 11
 LEAD = 2
 F32, BF16 = jnp.float32, jnp.bfloat16
 
@@ -19,7 +21,7 @@
     psi_hbm, left_hbm, right_hbm, out,
     left_ix, right_ix, mask, psi, left, half, part, got, mine, twin, full, *rest,
 ):
-    C = CHUNKS
+    C = len(CHUNKS)
     G = n_mpo // 2
     z_lo_size = n_sec // X
     ring = 2 * z_lo_size
@@ -27,10 +29,11 @@
     (in_sem, own_sem, r_send, r_recv, s_send, s_recv, z_send, z_recv, g_send, g_recv, far_sem) = rest[C:]
     W, S = left.shape[0], left.shape[1]
     B = psi.shape[-1]
-    lc = B // C
-    per = 128 // lc
-    groups = pairs // per
+    start = [sum(CHUNKS[:c]) for c in range(C)]
+    per = [128 // n for n in CHUNKS]
+    groups = [pairs // n for n in per]
     rows = B // G
+    order = sorted(range(1, G), key=lambda step: abs(step - G // 2))
 
     sec, mpo = lax.axis_index("sec"), lax.axis_index("mpo")
     z_hi, me = mpo // G, mpo % G
@@ -40,9 +43,13 @@
         z = lax.rem(z_hi * z_lo_size + z_lo + step + ring, ring)
         return lax.rem(z, z_lo_size) * X + x, (z // z_lo_size) * G + me
 
+    def some(c):
+        return pl.ds(0, groups[c])
+
     def in_plane(step):
         return sec, z_hi * G + lax.rem(me + step, G)
 
+    late = jnp.where(jnp.logical_and(z_lo >= FLIP, x == X - 1), 1 - z_hi, z_hi)
     has_low, has_high = sec > 0, sec < n_sec - 1
 
     def signal(sem, device):
@@ -55,11 +62,11 @@
         )
 
     barrier = pltpu.get_barrier_semaphore()
-    pl.when(z_hi == 0)(lambda: signal(barrier, along_z(ring // 2)))
     pl.when(has_low)(lambda: signal(barrier, (sec - 1, mpo)))
     pl.when(has_high)(lambda: signal(barrier, (sec + 1, mpo)))
-    for step in range(1, G):
+    for step in order:
         signal(barrier, in_plane(step))
+    pl.when(late == 0)(lambda: signal(barrier, along_z(ring // 2)))
 
     loads = [
         pltpu.make_async_copy(left_ix_hbm, left_ix, in_sem.at[2]),
@@ -69,18 +76,18 @@
         pltpu.make_async_copy(psi_hbm, psi, in_sem.at[1]),
     ]
     own = [
-        pltpu.make_async_copy(right_hbm.at[:, :, pl.ds(c * lc, lc)], wide[c].at[:, pl.ds(S, S)], own_sem.at[c])
+        pltpu.make_async_copy(right_hbm.at[:, :, pl.ds(start[c], CHUNKS[c])], wide[c].at[:, pl.ds(S, S)], own_sem.at[c])
         for c in range(C)
     ]
     for copy in loads + own:
         copy.start()
 
     def to_low(c):
-        return remote(right_hbm.at[:, :, pl.ds(c * lc, lc)], wide[c].at[:, pl.ds(2 * S, S)],
+        return remote(right_hbm.at[:, :, pl.ds(start[c], CHUNKS[c])], wide[c].at[:, pl.ds(2 * S, S)],
                       r_send.at[c, 0], r_recv.at[c, 0], (sec - 1, mpo))
 
     def to_high(c):
-        return remote(right_hbm.at[:, :, pl.ds(c * lc, lc)], wide[c].at[:, pl.ds(0, S)],
+        return remote(right_hbm.at[:, :, pl.ds(start[c], CHUNKS[c])], wide[c].at[:, pl.ds(0, S)],
                       r_send.at[c, 1], r_recv.at[c, 1], (sec + 1, mpo))
 
     def halves():
@@ -92,12 +99,11 @@
                 block = jnp.dot(left[w, left_at[p]], psi[p], preferred_element_type=F32)
                 half[w, p] = (block * mask[w, p].astype(F32)).astype(BF16)
 
-    pl.semaphore_wait(barrier, has_low.astype(jnp.int32) + has_high.astype(jnp.int32) + z_hi + (G - 1))
+    pl.semaphore_wait(barrier, has_low.astype(jnp.int32) + has_high.astype(jnp.int32) + late + (G - 1))
 
     for c in range(C):
         pl.when(has_low)(lambda c=c: to_low(c).start())
         pl.when(has_high)(lambda c=c: to_high(c).start())
-    pl.when(z_hi == 1)(lambda: signal(far_sem, along_z(ring // 2)))
     halves()
     first = sec * S
     right_at = [jnp.clip(right_ix[p] - first + S, 0, 3 * S - 1) for p in range(pairs)]
@@ -109,71 +115,71 @@
         pl.when(has_high)(lambda: to_low(c).wait_recv())
         pl.when(has_low)(lambda: to_high(c).wait_recv())
         lane = lax.broadcasted_iota(jnp.int32, (B, 128), 1)
-        for group in range(groups):
-            members = range(group * per, (group + 1) * per)
-            sums = [None] * per
+        for group in range(groups[c]):
+            members = range(group * per[c], (group + 1) * per[c])
+            sums = [None] * per[c]
             for w in range(W):
                 rights = jnp.concatenate([wide[c][w, right_at[p]] for p in members], axis=0)
                 for q, p in enumerate(members):
                     term = lax.dot_general(half[w, p], rights, (((1,), (1,)), ((), ())), preferred_element_type=F32)
                     sums[q] = term if sums[q] is None else sums[q] + term
             block = sums[0]
-            for q in range(1, per):
-                block = jnp.where(lane < q * lc, block, sums[q])
+            for q in range(1, per[c]):
+                block = jnp.where(lane < q * CHUNKS[c], block, sums[q])
             part[c, :, group] = block.astype(BF16).reshape(G, rows, 128)
-        for step in range(1, G):
-            copy = remote(part.at[c, lax.rem(me + step, G)], got.at[c, step - 1],
+        for step in order:
+            copy = remote(part.at[c, lax.rem(me + step, G), some(c)], got.at[c, step - 1, some(c)],
                           s_send.at[c, step - 1], s_recv.at[c, step - 1], in_plane(step))
             copy.start()
             sends.append(copy)
 
     def twin_copy(c):
-        return remote(mine.at[c], twin.at[c], z_send.at[c], z_recv.at[c], along_z(ring // 2))
+        return remote(mine.at[c, some(c)], twin.at[c, some(c)], z_send.at[c], z_recv.at[c], along_z(ring // 2))
 
     def add_up(c):
-        total = part[c, me].astype(F32)
-        for step in range(1, G):
-            remote(part.at[c, 0], got.at[c, step - 1], s_send.at[c, step - 1], s_recv.at[c, step - 1],
+        total = part[c, me, some(c)].astype(F32)
+        for step in order:
+            remote(part.at[c, 0, some(c)], got.at[c, step - 1, some(c)], s_send.at[c, step - 1], s_recv.at[c, step - 1],
                    in_plane(step)).wait_recv()
-            total = total + got[c, step - 1].astype(F32)
-        mine[c] = total.astype(BF16)
-        pl.when(z_hi == 1)(lambda: twin_copy(c).start())
+            total = total + got[c, step - 1, some(c)].astype(F32)
+        mine[c, some(c)] = total.astype(BF16)
+        pl.when(late == 1)(lambda: twin_copy(c).start())
 
     def hand_back(c):
         twin_copy(c).wait_recv()
         for k in range(C):
             if (k < LEAD and c == 0) or (k == c + LEAD - 1 and c > 0):
-                pl.when(jnp.logical_and(z_hi == 0, z_lo < REPLY))(lambda k=k: twin_copy(k).start())
-        full[c, me] = (mine[c].astype(F32) + twin[c].astype(F32)).astype(BF16)
-        for step in range(1, G):
-            copy = remote(full.at[c, me], full.at[c, me], g_send.at[c, step - 1], g_recv.at[c, step - 1], in_plane(step))
+                pl.when(jnp.logical_and(late == 0, z_lo < REPLY))(lambda k=k: twin_copy(k).start())
+        full[c, me, some(c)] = (mine[c, some(c)].astype(F32) + twin[c, some(c)].astype(F32)).astype(BF16)
+        for step in order:
+            copy = remote(full.at[c, me, some(c)], full.at[c, me, some(c)], g_send.at[c, step - 1], g_recv.at[c, step - 1], in_plane(step))
             copy.start()
             sends.append(copy)
 
     def place(c):
-        for step in range(1, G):
+        for step in order:
             source = lax.rem(me - step + G, G)
-            remote(full.at[c, source], full.at[c, source], g_send.at[c, step - 1], g_recv.at[c, step - 1],
+            remote(full.at[c, source, some(c)], full.at[c, source, some(c)], g_send.at[c, step - 1], g_recv.at[c, step - 1],
                    in_plane(step)).wait_recv()
-        if per == 1:
+        last = start[c] + CHUNKS[c]
+        if last % 128 == 0:
+            chunks = [k for k in range(c + 1) if start[k] >= last - 128]
             for p in range(pairs):
-                out[p, :, pl.ds(c * 128, 128)] = full[c, :, p].reshape(B, 128)
-        elif c % per == per - 1:
-            chunks = range(c - per + 1, c + 1)
-            for group in range(groups):
-                blocks = [full[k, :, group].reshape(B, 128) for k in chunks]
-                for q in range(per):
-                    out[group * per + q, :, pl.ds(c // per * 128, 128)] = jnp.concatenate(
-                        [b[:, q * lc:(q + 1) * lc] for b in blocks], axis=1
-                    )
+                blocks = [full[k, :, p // per[k]].reshape(B, 128) for k in chunks]
+                cuts = [(p % per[k]) * CHUNKS[k] for k in chunks]
+                out[p, :, pl.ds(last - 128, 128)] = jnp.concatenate(
+                    [b[:, i:i + CHUNKS[k]] for b, i, k in zip(blocks, cuts, chunks)], axis=1
+                )
 
     for c in range(C):
         contract(c)
+        if c == ANSWER:
+            pl.when(late == 1)(lambda: signal(far_sem, along_z(ring // 2)))
         if c > 0:
             add_up(c - 1)
     add_up(C - 1)
 
-    @pl.when(z_hi == 0)
+    @pl.when(late == 0)
     def _():
         pl.semaphore_wait(far_sem, 1)
 
@@ -200,11 +206,9 @@
     pairs, B, _ = wavefunction.shape
     W, S = left_env.shape[:2]
     G = n_mpo // 2
-    C = CHUNKS
-    lc = B // C
-    groups = pairs * lc // 128
+    C = len(CHUNKS)
     rows = B // G
-    piece = (groups, rows, 128)
+    piece = (max(pairs * n // 128 for n in CHUNKS), rows, 128)
     hbm = pl.BlockSpec(memory_space=pl.ANY)
     dma = pltpu.SemaphoreType.DMA
     return pl.pallas_call(
@@ -225,7 +229,7 @@
             pltpu.VMEM((C,) + piece, BF16),
             pltpu.VMEM((C, G) + piece, BF16),
         ]
-        + [pltpu.VMEM((W, 3 * S, lc, B), BF16)] * C
+        + [pltpu.VMEM((W, 3 * S, n, B), BF16) for n in CHUNKS]
         + [
             dma((5,)), dma((C,)), dma((C, 2)), dma((C, 2)),
             dma((C, G - 1)), dma((C, G - 1)), dma((C,)), dma((C,)),

time: 60.6 us -> 59.3 us (0.979)
  the two profiles are of different devices: /device:TPU:1 before, /device:TPU:33 now
where the time goes in v3:
time: 59.3 us; the launch traced here: 59.1 us
  Pallas kernels  58.3 us (98%)
  local copies, waits for them, and re-layouts  0.8 us (1%)
    pallas_call x1, Pallas kernels, per_device(): pl.pallas_call(functools.partial(kernel, n_sec, n_mpo, pairs), out_shape=...  58.3 us

profile of v3, /device:TPU:33, one launch (start us, length us, event | category | flops | bytes accessed | tf_op | source)
XLA Modules:
  0.0 59.1 jit_solution(17461624541845643419)
XLA Ops:
  0.0 58.3 %shard_map.64 = bf16[4,256,256]{2,1,0:T(8,128)(2,1)S(1)} custom-call(s32[4]{0:T(128)} %left_ix_hbm.1, s32[4]{0:T(128)} %right_ix_hbm.1, s32[2,4]{1,0:T(2,128)} %mask_hbm.1, bf16[4,256,256]{2,1,0:T(8,128)(2,1)} %psi_hbm.1, bf16[2,2,256,256]{3,2,1,0:T(8,128)(2,1)} %left_hbm.1, bf16[2,2,256,256]{3,2,1,0:T(8,128)(2,1)} %right_hbm.1), custom_call_target="tpu_custom_call" | custom-call | flops 536870912 | bytes 2097152 | tf_op jit(solution)/shard_map/pallas_call | solution.py:214
  58.3 0.8 %copy.8 = bf16[4,256,256]{2,1,0:T(8,128)(2,1)} copy(bf16[4,256,256]{2,1,0:T(8,128)(2,1)S(1)} %shard_map.64) | data formatting | bytes 1048576
